TPU v7x, 256 devices: a whole 4x4x8 slice. The times are simulated.
256 devices in a mesh: row: 8 (over y, z_hi), col: 32 (over x, z_lo, core).
Axes of the slice: x: 4, y: 4, z: 8 (z_hi: 2, z_lo: 4; z = z_hi * 4 + z_lo), core: 2. Of those that a mesh axis runs over, the one named last changes fastest.
Arguments:
- features: bfloat16 [65536, 256], P(('col', 'row')), may hold values from -6 to 6
- weight: bfloat16 [256, 256], replicated, may hold values from -0.375 to 0.375
- bias_vector: float32 [256], replicated, may hold values from -3 to 3
- adjacency_tiles: bfloat16 [8, 32, 24, 512, 512], P('row', 'col'), may hold values from -0.125 to 0.125
- tile_index: int32 [8, 32, 24], P('row', 'col'), may hold values from 0 to 63, as said below
- tile_count: int32 [8, 32], P('row', 'col'), may hold values from 1 to 24, as said below
- grad_output: bfloat16 [65536, 256], P(('row', 'col')), may hold values from -6 to 6
Outputs:
- output: bfloat16 [65536, 256], P(('row', 'col'))
- grad_features: bfloat16 [65536, 256], P(('col', 'row'))
- grad_weight: float32 [256, 256], replicated
- grad_bias: float32 [256], replicated
Inputs may be any that keep to these rules, and one draw needn't show every extreme that they name: `tile_index`: the 24 positions of one grid block are distinct. `tile_count`: slots of a grid block at or beyond its count hold arbitrary values that are not part of A and must be ignored.
All inputs are finite; a program needn't handle non-finite values.
Results may differ from a plain program's by a relative error of at most 0.0057.
Values may be sent and summed in bfloat16 or wider, within the bound.
A program may use at most 128 MiB of HBM per device.

v0:
```python
import math

import jax
import jax.numpy as jnp
from jax import lax
from jax.sharding import PartitionSpec as P


def silu_slope(shifted):
    sigma = jax.nn.sigmoid(shifted)
    return sigma * (1.0 + shifted * (1.0 - sigma))


def add_tiles(stacked, located, limit, source, out_rows, col_tiles, flipped):
    tile_size = stacked.shape[-1]

    def visit(position, running):
        matrix = lax.dynamic_index_in_dim(stacked, position, 0, keepdims=False)
        spot = lax.dynamic_index_in_dim(located, position, 0, keepdims=False)
        row_tile = spot // col_tiles
        col_tile = spot % col_tiles
        if flipped:
            piece = lax.dynamic_slice_in_dim(source, row_tile * tile_size, tile_size, 0)
            product = lax.dot_general(
                matrix, piece, (((0,), (0,)), ((), ())), preferred_element_type=jnp.float32
            )
            target = col_tile * tile_size
        else:
            piece = lax.dynamic_slice_in_dim(source, col_tile * tile_size, tile_size, 0)
            product = jnp.dot(matrix, piece, preferred_element_type=jnp.float32)
            target = row_tile * tile_size
        product = product * (position < limit).astype(jnp.float32)
        current = lax.dynamic_slice_in_dim(running, target, tile_size, 0)
        return lax.dynamic_update_slice_in_dim(running, current + product, target, 0)

    start = jnp.zeros((out_rows, source.shape[1]), jnp.float32)
    upper = stacked.shape[0]
    return lax.fori_loop(0, upper, visit, start)


def on_device(features, weight, bias_vector, adjacency_tiles, tile_index, tile_count, grad_output):
    node_rows = features.shape[0]
    tile_size = adjacency_tiles.shape[-1]
    row_count = lax.axis_size("row")
    col_count = lax.axis_size("col")
    stacked = adjacency_tiles[0, 0]
    located = tile_index[0, 0]
    limit = tile_count[0, 0]
    block_rows = node_rows * col_count
    block_cols = node_rows * row_count
    col_tiles = block_cols // tile_size
    mapped = jnp.dot(features, weight, preferred_element_type=jnp.float32).astype(jnp.bfloat16)
    panel = lax.all_gather(mapped, "row", axis=0, tiled=True)
    partial_rows = add_tiles(stacked, located, limit, panel, block_rows, col_tiles, False)
    whole = lax.psum(partial_rows, "col")
    shifted_all = whole + bias_vector[None, :]
    offset = lax.axis_index("col") * node_rows
    own_rows = lax.dynamic_slice_in_dim(shifted_all, offset, node_rows, 0)
    output = jax.nn.silu(own_rows).astype(jnp.bfloat16)
    cotangent_rows = lax.all_gather(grad_output, "col", axis=0, tiled=True)
    signal_rows = (cotangent_rows.astype(jnp.float32) * silu_slope(shifted_all)).astype(
        jnp.bfloat16
    )
    signal = lax.dynamic_slice_in_dim(signal_rows, offset, node_rows, 0)
    partial_cols = add_tiles(stacked, located, limit, signal_rows, block_cols, col_tiles, True)
    grad_mapped = lax.psum_scatter(partial_cols, "row", scatter_dimension=0, tiled=True)
    grad_features = jnp.dot(
        grad_mapped, weight.astype(jnp.float32).T, precision=lax.Precision.HIGHEST
    ).astype(jnp.bfloat16)
    scale = 1.0 / math.sqrt(node_rows * row_count * col_count)
    weight_term = (
        jnp.dot(features.astype(jnp.float32).T, grad_mapped, precision=lax.Precision.HIGHEST)
        * scale
    )
    bias_term = jnp.sum(signal.astype(jnp.float32), axis=0) * scale
    grad_weight, grad_bias = lax.psum((weight_term, bias_term), ("row", "col"))
    return (output, grad_features, grad_weight, grad_bias)


def solution(mesh):
    return jax.shard_map(
        on_device,
        mesh=mesh,
        in_specs=(
            P(("col", "row"), None),
            P(),
            P(),
            P("row", "col", None, None, None),
            P("row", "col", None),
            P("row", "col"),
            P(("row", "col"), None),
        ),
        out_specs=(P(("row", "col"), None), P(("col", "row"), None), P(), P()),
        check_vma=False,
    )
```

profile of v0, /device:TPU:8, one launch (start us, length us, event | category | flops | bytes accessed | tf_op | source)
XLA Modules:
  0.0 1030.7 jit_solution(14938521808474947347)
XLA Ops:
  8.1 1.7 convolution_convert_fusion.1
  10.6 65.1 %all-gather.3.cloned.1.call-done = bf16[2048,256]{1,0:T(8,128)(2,1)} async-done(((bf16[256,256]{1,0:T(8,128)(2,1)}), bf16[2048,256]{1,0:T(8,128)(2,1)}) %all-gather.3.cloned.1.call-update) | async-done | bytes 1048592 | tf_op jit(solution)/shard_map/all_gather | solution.py:53
  75.7 3.8 broadcast_in_dim.7
  79.5 149.9 %while.30 = (s32[]{:T(128)}, f32[8192,256]{1,0:T(8,128)}, s32[24]{0:T(128)S(1)}, bf16[24,512,512]{2,1,0:T(8,128)(2,1)}, bf16[2048,256]{1,0:T(8,128)(2,1)}, /*ind...) while((s32[]{:T(128)}, f32[8192,256]{1,0:T(8,128)}, ...), condition=%wide.region_1.2_spmd, body=%wide.region_0.1_spmd.sunk | while | flops 134479904 | bytes 1835478 | solution.py:38
  83.3 2.4 fusion.27
  89.6 2.4 fusion.27
  95.9 2.4 fusion.27
  102.2 2.4 fusion.27
  108.4 2.4 fusion.27
  114.7 2.4 fusion.27
  120.9 2.4 fusion.27
  127.1 2.4 fusion.27
  133.4 2.4 fusion.27
  139.6 2.4 fusion.27
  145.9 2.4 fusion.27
  152.1 2.4 fusion.27
  158.4 2.4 fusion.27
  164.6 2.4 fusion.27
  170.8 2.4 fusion.27
  177.1 2.4 fusion.27
  183.3 2.4 fusion.27
  189.6 2.4 fusion.27
  195.9 2.4 fusion.27
  202.1 2.4 fusion.27
  208.3 2.4 fusion.27
  214.6 2.4 fusion.27
  220.8 2.4 fusion.27
  227.1 2.4 fusion.27
  229.5 308.2 %all-reduce.3.cloned.1.call-done = f32[8192,256]{1,0:T(8,128)} async-done(((f32[8192,256]{1,0:T(8,128)}), f32[8192,256]{1,0:T(8,128)}) %all-reduce.3.cloned.1.call-update) | async-done | bytes 8388624 | tf_op jit(solution)/shard_map/psum | solution.py:55
  537.7 9.0 multiply_convert_fusion
  546.9 128.5 %while.31 = (s32[]{:T(128)}, f32[2048,256]{1,0:T(8,128)S(1)}, s32[24]{0:T(128)S(1)}, bf16[24,512,512]{2,1,0:T(8,128)(2,1)}, bf16[8192,256]{1,0:T(8,128)(2,1)}, /...) while((s32[]{:T(128)}, f32[2048,256]{1,0:T(8,128)S(1)}, ...), condition=%wide.region_4.5_spmd, body=%wide.region_3.4_spmd.sunk | while | flops 134479904 | bytes 1835478 | solution.py:38
  550.7 1.5 fusion.30
  556.1 1.5 fusion.30
  566.8 1.5 fusion.30
  572.2 1.5 fusion.30
  582.9 1.5 fusion.30
  598.9 1.5 fusion.30
  615.0 1.5 fusion.30
  631.0 1.5 fusion.30
  647.1 1.5 fusion.30
  663.2 1.5 fusion.30
  677.8 77.8 %psum.23 = f32[256]{0:T(256)} all-reduce(f32[256]{0:T(256)S(1)} %broadcast_multiply_fusion), channel_id=1, replica_groups=mesh['row'=8,'col'=32] {'row','col'}, use_global_device_ids=true, to_apply=%region_8.9 | all-reduce | flops 256 | bytes 2048 | tf_op jit(solution)/shard_map/psum | solution.py:76
  755.6 1.7 multiply_convert_fusion.1
  757.2 12.3 %reduce-scatter.2.cloned.1.call-done = f32[256,256]{1,0:T(8,128)} async-done(((f32[2048,256]{1,0:T(8,128)}), f32[256,256]{1,0:T(8,128)}) %reduce-scatter.2.cloned.1.call-update) | async-done | bytes 262160 | tf_op jit(solution)/shard_map/reduce_scatter | solution.py:66
  769.6 2.0 fusion.12
  771.6 2.0 convolution_convert_fusion
  773.6 248.8 %all-reduce.5.cloned.1.call-done = f32[256,256]{0,1:T(8,128)} async-done(((f32[256,256]{0,1:T(8,128)}), f32[256,256]{0,1:T(8,128)}) %all-reduce.5.cloned.1.call-update) | async-done | bytes 262160 | tf_op jit(solution)/shard_map/psum | solution.py:76
  1022.4 1.8 copy.11
  (86 shorter events, 53.0 us)
Async XLA Ops:
  7.2 0.9 copy-start
  7.2 72.3 %copy-start.4 = (s32[1,1,24]{2,1,0:T(1,128)S(1)}, s32[1,1,24]{2,1,0:T(1,128)}, u32[]{:S(2)}) copy-start(s32[1,1,24]{2,1,0:T(1,128)} %param.15) | copy-start | bytes 292
  7.2 68.5 %all-gather.3.cloned.1.call-start = ((), (), s32[]{:S(2)}) async-start(), calls=%async_computation.1 | async-start | bytes 1179648 | tf_op jit(solution)/shard_map/all_gather | solution.py:53
  9.9 219.7 %all-gather.5.cloned.1.call-start = ((), (), s32[]{:S(2)}) async-start(), calls=%async_computation.3 | async-start | bytes 4325376 | tf_op jit(solution)/shard_map/all_gather | solution.py:60
  10.6 527.1 %all-reduce.3.cloned.1.call-start = ((), (), s32[]{:S(2)}) async-start(), calls=%async_computation.2 | async-start | bytes 16777216 | tf_op jit(solution)/shard_map/psum | solution.py:55
  79.5 458.2 %copy-start.3 = (f32[256]{0:T(256)S(1)}, f32[256]{0:T(256)}, u32[]{:S(2)}) copy-start(f32[256]{0:T(256)} %param.13) | copy-start | bytes 3076
  229.5 540.1 %reduce-scatter.2.cloned.1.call-start = ((), (), s32[]{:S(2)}) async-start(), calls=%async_computation.4 | async-start | bytes 2359296 | tf_op jit(solution)/shard_map/reduce_scatter | solution.py:66
  546.7 224.9 %copy-start.2 = (bf16[256,256]{1,0:T(8,128)(2,1)S(1)}, bf16[256,256]{1,0:T(8,128)(2,1)}, u32[]{:S(2)}) copy-start(bf16[256,256]{1,0:T(8,128)(2,1)} %param.12) | copy-start | bytes 393220
  675.3 1.4 copy-start.1
  676.7 345.7 %all-reduce.5.cloned.1.call-start = ((), (), s32[]{:S(2)}) async-start(), calls=%async_computation.5 | async-start | bytes 524288 | tf_op jit(solution)/shard_map/psum | solution.py:76
Sparse Core Ops, SparseCore 0:
  11.2 64.4 all-gather.2
  77.6 59.0 all-gather.4
  229.6 308.0 all-reduce.2
  676.9 92.6 reduce-scatter.1
  776.3 246.0 all-reduce.4
where the time goes:
time: 1030 us
  waiting for transfers between devices  635 us (62%)
  loops' own time  158 us (15%)
  matrix products  98.6 us (10%)
  blocking collectives  77.8 us (8%)
  local copies, waits for them, and re-layouts  36 us (3%)
  between operations  13.8 us (1%)
  other arithmetic  11.7 us (1%)
    psum x1, waiting for transfers between devices, on_device(): whole = lax.psum(partial_rows, 'col')  308 us
    psum x1, waiting for transfers between devices, on_device(): grad_weight, grad_bias = lax.psum((weight_term, bias_term), ('row', 'col'))  249 us
    another operation x2, loops' own time, add_tiles(): return lax.fori_loop(0, upper, visit, start)  158 us
    psum x1, blocking collectives, on_device(): grad_weight, grad_bias = lax.psum((weight_term, bias_term), ('row', 'col'))  77.8 us
    all_gather x1, waiting for transfers between devices, on_device(): panel = lax.all_gather(mapped, 'row', axis=0, tiled=True)  65.1 us
    dot_general x24, matrix products, visit(): product = jnp.dot(matrix, piece, preferred_element_type=jnp.float32)  57.5 us
    dot_general x24, matrix products, visit(): lax.dot_general(matrix, piece, (((0,), (0,)), ((), ())), preferred_elemen...  35.4 us
    dynamic_slice x48, local copies, waits for them, and re-layouts, visit(): spot = lax.dynamic_index_in_dim(located, position, 0, keepdims=False)  28 us
  transfers between devices with their start and end apart: 5, of which 4 were waited for; matrix products, arithmetic and copies ran while one was open for 8% of the time, Pallas kernels for 0%

commit v1 on v0

v1 whole, which is shorter than its diff:
```python
import math

import jax
import jax.numpy as jnp
from jax import lax
from jax.experimental import pallas as pl
from jax.experimental.pallas import tpu as pltpu
from jax.sharding import PartitionSpec as P

MESH = pl.DeviceIdType.MESH
F32 = jnp.float32
BF16 = jnp.bfloat16
N = 256
HALF = 128
TILE = 512
SLOTS = 24
LOADS = 8


def pick(index, options):
    value = options[-1]
    for place in range(len(options) - 2, -1, -1):
        value = jnp.where(index == place, options[place], value)
    return value


def order_far_first(j, z):
    low = jnp.where(z < 2, z, 3 - z)
    base = jnp.where(low == 0, 3 - j, pick(j, [3, 0, 2, 1]))
    return jnp.where(z < 2, base, 3 - base)


def order_near_first(j, z):
    low = jnp.where(z < 2, z, 3 - z)
    base = jnp.where(low == 0, j, pick(j, [1, 0, 2, 3]))
    return jnp.where(z < 2, base, 3 - base)


def split_dot(left, right, dims):
    high = left.astype(BF16)
    low = (left - high.astype(F32)).astype(BF16)
    return lax.dot_general(high, right, dims, preferred_element_type=F32) + lax.dot_general(
        low, right, dims, preferred_element_type=F32
    )


def kernel(
    slots, features, weight, bias, tiles_hbm, cotangent,
    output, grad_features, grad_weight, grad_bias,
    tiles, feat, pair_out, pair_in, own, xa, xb, xc, xra, xrb, xrc, zs, zr,
    sig, acc, ya, yb, yc, yra, yrb, yrc, qs, qr,
    wa, wra, wk, wx, wz, wg, work,
    load_sem, fy_s, fy_r, fh_s, fh_r, pair_s, pair_r, x_s, x_r, z_s, z_r,
    gp_s, gp_r, gx_s, gx_r, gz_s, gz_r, y_s, y_r, q_s, q_r,
    wa_s, wa_r, wk_s, wk_r, wx_s, wx_r, wz_s, wz_r, wg_s, wg_r,
):
    row, col = lax.axis_index("row"), lax.axis_index("col")
    y, h = row // 2, row % 2
    x, z, k = col // 8, (col // 2) % 4, col % 2
    other = 1 - k
    scale = 1.0 / math.sqrt(65536)

    def column(xx, zz, kk):
        return (xx * 4 + zz) * 2 + kk

    def remote(src, dst, send, recv, to_row, to_col):
        return pltpu.make_async_remote_copy(
            src_ref=src, dst_ref=dst, send_sem=send, recv_sem=recv,
            device_id=(to_row, to_col), device_id_type=MESH,
        )

    x_next = [column((x + 1) % 4, z, k), column((x + 3) % 4, z, k)]
    y_next = [((y + 1) % 4) * 2 + h, ((y + 3) % 4) * 2 + h]
    z_up = column(x, jnp.minimum(z + 1, 3), k)
    z_down = column(x, jnp.maximum(z - 1, 0), k)
    z_next = [z_up, z_down]
    twin = column(x, z, other)
    across = y * 2 + 1 - h
    edge = (z == 0) | (z == 3)

    def rows(half):
        return pl.ds(half * HALF, HALF)

    barrier = pltpu.get_barrier_semaphore()
    partners = [(row, twin)]
    for step in range(1, 4):
        partners.append((row, column((x + step) % 4, z, k)))
        partners.append((row, column(x, (z + step) % 4, k)))
    for step in range(1, 8):
        partners.append(((row + step) % 8, col))
    for to_row, to_col in partners:
        pl.semaphore_signal(barrier, inc=1, device_id=(to_row, to_col), device_id_type=MESH)

    def tile_load(part):
        count = SLOTS // LOADS
        return pltpu.make_async_copy(
            tiles_hbm.at[pl.ds(part * count, count)], tiles.at[pl.ds(part * count, count)], load_sem.at[part]
        )

    for part in range(LOADS):
        tile_load(part).start()
    tiles[SLOTS] = jnp.zeros((TILE, TILE), BF16)
    acc[...] = jnp.zeros(acc.shape, F32)
    mine = pl.ds(row * N, N)
    feat[mine, :] = features[...]
    pl.semaphore_wait(barrier, len(partners))

    def feat_rows(yy, hh, half):
        return feat.at[pl.ds((yy * 2 + hh) * N + half * HALF, HALF)]

    def feat_across(half):
        here = feat_rows(y, h, half)
        return remote(here, here, fh_s.at[half], fh_r.at[half], across, col)

    def feat_across_in(half):
        there = feat_rows(y, 1 - h, half)
        return remote(there, there, fh_s.at[half], fh_r.at[half], across, col)

    def feat_y(kind, way, g):
        hh = h if g == 0 else 1 - h
        behind = (y + (3 if way == 0 else 1)) % 4
        block = feat_rows(behind if kind == 2 else y, hh, way if kind != 1 else 1 - way)
        return remote(block, block, fy_s.at[kind, way, g], fy_r.at[kind, way, g], y_next[way], col)

    def feat_y_in(kind, way, g):
        hh = h if g == 0 else 1 - h
        behind = (y + (3 if way == 0 else 1)) % 4
        source = (y + 2) % 4 if kind == 2 else behind
        block = feat_rows(source, hh, way if kind != 1 else 1 - way)
        return remote(block, block, fy_s.at[kind, way, g], fy_r.at[kind, way, g], y_next[way], col)

    for half in range(2):
        feat_across(half).start()
    for kind in range(2):
        for way in range(2):
            feat_y(kind, way, 0).start()
    for way in range(2):
        feat_y_in(0, way, 0).wait_recv()
        feat_y(2, way, 0).start()
    for half in range(2):
        feat_across_in(half).wait_recv()
        feat_y(0, half, 1).start()
        feat_y(1, 1 - half, 1).start()
    for way in range(2):
        feat_y_in(0, way, 1).wait_recv()
        feat_y(2, way, 1).start()
    for g in range(2):
        for way in range(2):
            feat_y_in(1, way, g).wait_recv()
            feat_y_in(2, way, g).wait_recv()
    for part in range(LOADS):
        tile_load(part).wait()

    def pair_copy(u):
        return remote(pair_out.at[u], pair_in.at[u], pair_s.at[u], pair_r.at[u], row, twin)

    def x_copy(kind, way, j):
        if kind == 0:
            src, dst = xa.at[j, rows(way)], xra.at[way, j]
        elif kind == 1:
            src, dst = xb.at[way, j], xrb.at[way, j]
        else:
            src, dst = xc.at[way, j], xrc.at[way, j]
        return remote(src, dst, x_s.at[kind, way, j], x_r.at[kind, way, j], row, x_next[way])

    def z_copy(j):
        target = order_far_first(j, z)
        way = jnp.where(target > z, 0, 1)
        to = jnp.where(target > z, z_up, z_down)
        return remote(zs.at[j], zr.at[way, target], z_s.at[j], z_r.at[way, target], row, to)

    def z_wait(way, target):
        block = zr.at[way, target]
        remote(zs.at[0], block, z_s.at[0], z_r.at[way, target], row, twin).wait_recv()

    def forward_half(t, k_half):
        total = None
        for c in range(4):
            part = jnp.dot(
                tiles[slots[t * 4 + c], pl.ds(k_half * N, N), :],
                feat[c * TILE : (c + 1) * TILE, :],
                preferred_element_type=F32,
            )
            total = part if total is None else total + part
        return total

    def forward_step(s, carry):
        @pl.when(s < 16)
        def _():
            xx = (x + pick(s % 4, [2, 1, 3, 0])) % 4
            t = xx * 4 + order_far_first(s // 4, z)
            pair_out[s] = forward_half(t, other).astype(BF16)
            pair_copy(s).start()
            own[s] = forward_half(t, k)

        @pl.when((s >= 1) & (s <= 16))
        def _():
            u = s - 1
            j = u // 4
            pair_copy(u).wait_recv()

            @pl.when(u % 4 == 0)
            def _():
                xa[j] = (own[u] + pair_in[u].astype(F32)).astype(BF16)
                x_copy(0, 0, j).start()
                x_copy(0, 1, j).start()

            for way in range(2):

                @pl.when(u % 4 == 1 + way)
                def _():
                    far, near = rows(way), rows(1 - way)
                    xb[way, j] = (own[u, near, :] + pair_in[u, near, :].astype(F32)).astype(BF16)
                    x_copy(1, way, j).start()
                    own[u, far, :] = own[u, far, :] + pair_in[u, far, :].astype(F32)

            @pl.when(u % 4 == 3)
            def _():
                own[u] = own[u] + pair_in[u].astype(F32)

        @pl.when((s % 4 == 0) & (s >= 4) & (s <= 16))
        def _():
            j = s // 4 - 1
            for way in range(2):
                x_copy(0, way, j).wait_recv()
                xc[way, j] = (own[4 * j + 1 + way, rows(way), :] + xra[way, j].astype(F32)).astype(BF16)
                x_copy(2, way, j).start()

        @pl.when((s % 4 == 3) & (s >= 7))
        def _():
            j = (s - 7) // 4
            u = 4 * j + 3
            for way in range(2):
                x_copy(1, way, j).wait_recv()
                x_copy(2, way, j).wait_recv()
            for half in range(2):
                own[u, rows(half), :] = (
                    own[u, rows(half), :] + xrc[half, j].astype(F32) + xrb[1 - half, j].astype(F32)
                )

            @pl.when(edge & (j < 3))
            def _():
                zs[j] = own[u].astype(BF16)
                z_copy(j).start()

            def middle(jj):
                target = order_far_first(jj, z)
                way = jnp.where(target > z, 0, 1)
                z_wait(way, target)
                zs[jj] = (own[4 * jj + 3] + zr[way, target].astype(F32)).astype(BF16)
                z_copy(jj).start()

            @pl.when(jnp.logical_not(edge) & (j == 1))
            def _():
                middle(0)

            @pl.when(jnp.logical_not(edge) & (j == 2))
            def _():
                middle(1)
                middle(2)

        return carry

    lax.fori_loop(0, 20, forward_step, 0)

    @pl.when(z > 0)
    def _():
        z_wait(0, z)
        own[15] = own[15] + zr[0, z].astype(F32)

    @pl.when(z < 3)
    def _():
        z_wait(1, z)
        own[15] = own[15] + zr[1, z].astype(F32)

    gathered = own[15]
    shifted = split_dot(gathered, weight[...], (((1,), (0,)), ((), ()))) + bias[...]
    sigma = jax.nn.sigmoid(shifted)
    output[...] = (shifted * sigma).astype(BF16)
    signal = (cotangent[...].astype(F32) * (sigma * (1.0 + shifted * (1.0 - sigma)))).astype(BF16)
    work[...] = signal
    sig[x * 4 + z, k] = signal.astype(F32).T.astype(BF16)

    def sig_pair(t, kk):
        block = sig.at[t, kk]
        return remote(block, block, gp_s.at[t], gp_r.at[t], row, twin)

    def sig_z(way, piece):
        block = sig.at[x * 4 + piece, k]
        return remote(block, block, gz_s.at[way, piece], gz_r.at[way, piece], row, z_next[way])

    def sig_x(kind, way, j, arriving=False):
        piece = order_near_first(j, z)
        behind = (x + (3 if way == 0 else 1)) % 4
        if arriving:
            source = (x + 2) % 4 if kind == 2 else behind
        else:
            source = behind if kind == 2 else x
        block = sig.at[source * 4 + piece, k, rows(way if kind != 1 else 1 - way)]
        return remote(block, block, gx_s.at[kind, way, j], gx_r.at[kind, way, j], row, x_next[way])

    def launch_piece(j):
        for kind in range(2):
            for way in range(2):
                sig_x(kind, way, j).start()
        sig_pair(x * 4 + order_near_first(j, z), k).start()

    @pl.when(z < 3)
    def _():
        sig_z(0, z).start()

    @pl.when(z > 0)
    def _():
        sig_z(1, z).start()

    launch_piece(0)

    def wa_copy(peer):
        return remote(wa.at[peer], wra.at[row], wa_s.at[peer], wa_r.at[row], peer, col)

    def wa_in(peer):
        return remote(wa.at[peer], wra.at[peer], wa_s.at[peer], wa_r.at[peer], peer, col)

    part = split_dot(gathered.T, work[...], (((1,), (0,)), ((), ())))
    bias_part = jnp.sum(work[...].astype(F32), axis=0, keepdims=True)
    bias_rows = jnp.where(lax.broadcasted_iota(jnp.int32, (8, N), 0) == 0, jnp.broadcast_to(bias_part, (8, N)), 0.0)
    for peer in range(8):
        wa[peer, 0:32, :] = part[peer * 32 : (peer + 1) * 32, :]
        wa[peer, 32:40, :] = bias_rows
    wra[row] = wa[row]
    for step in range(1, 8):
        wa_copy((row + step) % 8).start()

    def wk_copy(here):
        return remote(wk.at[here], wk.at[here], wk_s.at[0], wk_r.at[0], row, twin)

    def wx_copy(here, to):
        return remote(wx.at[here], wx.at[here], wx_s.at[to], wx_r.at[here], row, column(to, z, k))

    def wz_copy(here, to):
        return remote(wz.at[here], wz.at[here], wz_s.at[to], wz_r.at[here], row, column(x, to, k))

    def wg_copy(here, to):
        return remote(wg.at[here], wg.at[here], wg_s.at[to], wg_r.at[here], to, col)

    def total_of(ref, count):
        total = ref[0]
        for place in range(1, count):
            total = total + ref[place]
        return total

    def weights_rows():
        for step in range(1, 8):
            wa_in((row + step) % 8).wait_recv()
        wk[k] = total_of(wra, 8)
        wk_copy(k).start()

    def weights_pair():
        wk_copy(other).wait_recv()
        wx[x] = total_of(wk, 2)
        for step in range(1, 4):
            wx_copy(x, (x + step) % 4).start()

    def weights_x():
        for step in range(1, 4):
            wx_copy((x + step) % 4, (x + step) % 4).wait_recv()
        wz[z] = total_of(wx, 4)
        for step in range(1, 4):
            wz_copy(z, (z + step) % 4).start()

    def weights_z():
        for step in range(1, 4):
            wz_copy((z + step) % 4, (z + step) % 4).wait_recv()
        wg[row] = total_of(wz, 4) * scale
        for step in range(1, 8):
            wg_copy(row, (row + step) % 8).start()

    def backward_step(s, carry):
        j = s // 4
        live = s < 16

        @pl.when(live & (s % 4 == 0))
        def _():
            for way in range(2):
                sig_x(0, way, j, True).wait_recv()
                sig_x(2, way, j).start()

        @pl.when((s % 4 == 1) & (s < 12))
        def _():
            jj = j + 1
            piece = order_near_first(jj, z)

            @pl.when(z == 0)
            def _():
                sig_z(1, piece).wait_recv()

            @pl.when(z == 3)
            def _():
                sig_z(0, piece).wait_recv()

            @pl.when(jnp.logical_not(edge) & (jj == 1))
            def _():
                sig_z(0, z - 1).wait_recv()
                sig_z(0, z - 1).start()
                sig_z(1, z + 1).wait_recv()
                sig_z(1, z + 1).start()

            @pl.when((z == 1) & (jj == 2))
            def _():
                sig_z(1, 3).wait_recv()
                sig_z(1, 3).start()

            @pl.when((z == 2) & (jj == 2))
            def _():
                sig_z(0, 0).wait_recv()
                sig_z(0, 0).start()

            launch_piece(jj)

        @pl.when(live & (s % 4 == 2))
        def _():
            piece = order_near_first(j, z)
            for way in range(2):
                sig_x(1, way, j, True).wait_recv()
                sig_pair(((x + (3 if way == 0 else 1)) % 4) * 4 + piece, k).start()

        @pl.when(live & (s % 4 == 3))
        def _():
            for way in range(2):
                sig_x(2, way, j, True).wait_recv()
            sig_pair(((x + 2) % 4) * 4 + order_near_first(j, z), k).start()

        for when, what in ((4, weights_rows), (7, weights_pair), (10, weights_x), (14, weights_z)):

            @pl.when(s == when)
            def _(what=what):
                what()

        @pl.when(s >= 2)
        def _():
            u = s - 2
            t = ((x + pick(u % 4, [0, 3, 1, 2])) % 4) * 4 + order_near_first(u // 4, z)
            sig_pair(t, other).wait_recv()
            for c in range(4):
                slot = slots[t * 4 + c]
                part = jnp.dot(sig[t, 0], tiles[slot, 0:N, :], preferred_element_type=F32) + jnp.dot(
                    sig[t, 1], tiles[slot, N:TILE, :], preferred_element_type=F32
                )
                acc[c, 0] += part[:, 0:N]
                acc[c, 1] += part[:, N:TILE]

        return carry

    lax.fori_loop(0, 18, backward_step, 0)

    def y_copy(kind, way, g):
        if kind == 0:
            src, dst = ya.at[g, rows(way)], yra.at[way, g]
        elif kind == 1:
            src, dst = yb.at[way, g], yrb.at[way, g]
        else:
            src, dst = yc.at[way, g], yrc.at[way, g]
        return remote(src, dst, y_s.at[kind, way, g], y_r.at[kind, way, g], y_next[way], col)

    def y_open(g):
        hh = 1 - h if g == 0 else h
        ya[g] = acc[(y + 2) % 4, hh].astype(BF16)
        for way in range(2):
            y_copy(0, way, g).start()
        for way in range(2):
            yb[way, g] = acc[(y + (1 if way == 0 else 3)) % 4, hh, rows(1 - way), :].astype(BF16)
            y_copy(1, way, g).start()

    def y_relay(g):
        hh = 1 - h if g == 0 else h
        for way in range(2):
            y_copy(0, way, g).wait_recv()
            near = acc[(y + (1 if way == 0 else 3)) % 4, hh, rows(way), :]
            yc[way, g] = (near + yra[way, g].astype(F32)).astype(BF16)
            y_copy(2, way, g).start()

    def y_close(g):
        hh = 1 - h if g == 0 else h
        for way in range(2):
            y_copy(1, way, g).wait_recv()
            y_copy(2, way, g).wait_recv()
        for half in range(2):
            acc[y, hh, rows(half), :] = (
                acc[y, hh, rows(half), :] + yrc[half, g].astype(F32) + yrb[1 - half, g].astype(F32)
            )

    def q_copy(half):
        return remote(qs.at[half], qr.at[half], q_s.at[half], q_r.at[half], across, col)

    y_open(0)
    y_relay(0)
    y_open(1)
    y_close(0)
    for half in range(2):
        qs[half] = acc[y, 1 - h, rows(half), :].astype(BF16)
        q_copy(half).start()
    y_relay(1)
    for step in range(1, 8):
        wg_copy((row + step) % 8, (row + step) % 8).wait_recv()
    for peer in range(8):
        grad_weight[peer * 32 : (peer + 1) * 32, :] = wg[peer, 0:32, :]
    grad_bias[...] = wg[0, 32:40, :]
    y_close(1)
    for half in range(2):
        q_copy(half).wait_recv()
        acc[y, h, rows(half), :] = acc[y, h, rows(half), :] + qr[half].astype(F32)
    grad_features[...] = split_dot(acc[y, h].T, weight[...], (((1,), (1,)), ((), ()))).astype(BF16)

    for half in range(2):
        feat_across(half).wait_send()
        q_copy(half).wait_send()
    for kind in range(3):
        for way in range(2):
            for g in range(2):
                feat_y(kind, way, g).wait_send()
                y_copy(kind, way, g).wait_send()

    def sent_pair(u, carry):
        pair_copy(u).wait_send()
        sig_pair(u, k).wait_send()
        return carry

    lax.fori_loop(0, 16, sent_pair, 0)

    def sent_x(j, carry):
        for kind in range(3):
            for way in range(2):
                x_copy(kind, way, j).wait_send()
                sig_x(kind, way, j).wait_send()
        return carry

    lax.fori_loop(0, 4, sent_x, 0)
    for j in range(3):
        z_copy(j).wait_send()
    for piece in range(4):

        @pl.when((z < 3) & (piece <= z))
        def _():
            sig_z(0, piece).wait_send()

        @pl.when((z > 0) & (piece >= z))
        def _():
            sig_z(1, piece).wait_send()

    for step in range(1, 8):
        wa_copy((row + step) % 8).wait_send()
        wg_copy(row, (row + step) % 8).wait_send()
    wk_copy(k).wait_send()
    for step in range(1, 4):
        wx_copy(x, (x + step) % 4).wait_send()
        wz_copy(z, (z + step) % 4).wait_send()


def on_device(features, weight, bias_vector, adjacency_tiles, tile_index, tile_count, grad_output):
    located = tile_index[0, 0]
    places = jnp.arange(SLOTS, dtype=jnp.int32)[:, None]
    hit = (located[:, None] == jnp.arange(64, dtype=jnp.int32)[None, :]) & (places < tile_count[0, 0])
    slots = jnp.min(jnp.where(hit, places, SLOTS), axis=0)
    vmem = pl.BlockSpec(memory_space=pltpu.VMEM)
    dma = pltpu.SemaphoreType.DMA
    output, grad_features, grad_weight, grad_bias = pl.pallas_call(
        kernel,
        out_shape=(
            jax.ShapeDtypeStruct((N, N), BF16),
            jax.ShapeDtypeStruct((N, N), BF16),
            jax.ShapeDtypeStruct((N, N), F32),
            jax.ShapeDtypeStruct((8, N), F32),
        ),
        in_specs=[
            pl.BlockSpec(memory_space=pltpu.SMEM), vmem, vmem, vmem, pl.BlockSpec(memory_space=pl.ANY), vmem,
        ],
        out_specs=(vmem, vmem, vmem, vmem),
        scratch_shapes=[
            pltpu.VMEM((SLOTS + 1, TILE, TILE), BF16),
            pltpu.VMEM((8 * N, N), BF16),
            pltpu.VMEM((16, N, N), BF16),
            pltpu.VMEM((16, N, N), BF16),
            pltpu.VMEM((16, N, N), F32),
            pltpu.VMEM((4, N, N), BF16),
            pltpu.VMEM((2, 4, HALF, N), BF16),
            pltpu.VMEM((2, 4, HALF, N), BF16),
            pltpu.VMEM((2, 4, HALF, N), BF16),
            pltpu.VMEM((2, 4, HALF, N), BF16),
            pltpu.VMEM((2, 4, HALF, N), BF16),
            pltpu.VMEM((3, N, N), BF16),
            pltpu.VMEM((2, 4, N, N), BF16),
            pltpu.VMEM((16, 2, N, N), BF16),
            pltpu.VMEM((4, 2, N, N), F32),
            pltpu.VMEM((2, N, N), BF16),
            pltpu.VMEM((2, 2, HALF, N), BF16),
            pltpu.VMEM((2, 2, HALF, N), BF16),
            pltpu.VMEM((2, 2, HALF, N), BF16),
            pltpu.VMEM((2, 2, HALF, N), BF16),
            pltpu.VMEM((2, 2, HALF, N), BF16),
            pltpu.VMEM((2, HALF, N), BF16),
            pltpu.VMEM((2, HALF, N), BF16),
            pltpu.VMEM((8, 40, N), F32),
            pltpu.VMEM((8, 40, N), F32),
            pltpu.VMEM((2, 40, N), F32),
            pltpu.VMEM((4, 40, N), F32),
            pltpu.VMEM((4, 40, N), F32),
            pltpu.VMEM((8, 40, N), F32),
            pltpu.VMEM((N, N), BF16),
            dma((LOADS,)),
            dma((3, 2, 2)), dma((3, 2, 2)), dma((2,)), dma((2,)),
            dma((16,)), dma((16,)), dma((3, 2, 4)), dma((3, 2, 4)), dma((3,)), dma((2, 4)),
            dma((16,)), dma((16,)), dma((3, 2, 4)), dma((3, 2, 4)), dma((2, 4)), dma((2, 4)),
            dma((3, 2, 2)), dma((3, 2, 2)), dma((2,)), dma((2,)),
            dma((8,)), dma((8,)), dma((1,)), dma((1,)), dma((4,)), dma((4,)), dma((4,)), dma((4,)),
            dma((8,)), dma((8,)),
        ],
        compiler_params=pltpu.CompilerParams(
            collective_id=0, has_side_effects=True, vmem_limit_bytes=56 * 1024 * 1024
        ),
        name="graph_layer",
    )(slots, features, weight, bias_vector[None, :], adjacency_tiles[0, 0], grad_output)
    return output, grad_features, grad_weight, grad_bias[0]


def solution(mesh):
    return jax.shard_map(
        on_device,
        mesh=mesh,
        in_specs=(
            P(("col", "row"), None),
            P(),
            P(),
            P("row", "col", None, None, None),
            P("row", "col", None),
            P("row", "col"),
            P(("row", "col"), None),
        ),
        out_specs=(P(("row", "col"), None), P(("col", "row"), None), P(), P()),
        check_vma=False,
    )
```

time: 1030 us -> 117 us (0.11)
  waiting for transfers between devices: 635 us -> 0 us
  loops' own time: 158 us -> 0 us
  Pallas kernels: 0 us -> 106 us
  matrix products: 98.6 us -> 0 us
  blocking collectives: 77.8 us -> 0 us
  local copies, waits for them, and re-layouts: 36 us -> 6.06 us
  between operations: 13.8 us -> 1.29 us
  other arithmetic: 11.7 us -> 1.26 us
    psum x2 -> x0, waiting for transfers between devices: 557 us -> none  [the longest x1 308 us: on_device(): whole = lax.psum(partial_rows, 'col')]
    another operation x2 -> x0, loops' own time: 158 us -> none  [add_tiles(): return lax.fori_loop(0, upper, visit, start)]
    pallas_call x0 -> x1, Pallas kernels: none -> 106 us  [on_device(): pl.pallas_call(kernel, out_shape=(jax.ShapeDtypeStruct((N, N), BF16), jax...]
    dot_general x51 -> x0, matrix products: 98.6 us -> none  [the longest x24 57.5 us: visit(): product = jnp.dot(matrix, piece, preferred_element_type=jnp.float32)]
    psum x1 -> x0, blocking collectives: 77.8 us -> none  [on_device(): grad_weight, grad_bias = lax.psum((weight_term, bias_term), ('row', 'col'))]
    all_gather x2 -> x0, waiting for transfers between devices: 65.1 us -> none  [the longest x1 65.1 us: on_device(): panel = lax.all_gather(mapped, 'row', axis=0, tiled=True)]
    dynamic_slice x48 -> x0, local copies, waits for them, and re-layouts: 28 us -> none  [visit(): spot = lax.dynamic_index_in_dim(located, position, 0, keepdims=False)]
    reduce_scatter x1 -> x0, waiting for transfers between devices: 12.3 us -> none  [on_device(): lax.psum_scatter(partial_cols, 'row', scatter_dimension=0, tiled=True)]
  transfers between devices with their start and end apart: 5 -> 0, of which waited for: 4 -> 0; matrix products, arithmetic and copies ran while one was open for 8% -> 0% of each run, Pallas kernels for 0% -> 0%
where the time goes in v1:
time: 117 us; the launch traced here: 115 us
  Pallas kernels  106 us (91%)
  local copies, waits for them, and re-layouts  6.06 us (5%)
  between operations  1.29 us (1%)
  other arithmetic  1.26 us (1%)
    pallas_call x1, Pallas kernels, on_device(): pl.pallas_call(kernel, out_shape=(jax.ShapeDtypeStruct((N, N), BF16), jax...  106 us
    unnamed x3, local copies, waits for them, and re-layouts  4.8 us

profile of v1, /device:TPU:8, one launch (start us, length us, event | category | flops | bytes accessed | tf_op | source)
XLA Modules:
  0.0 114.7 jit_solution(17174074051399576819)
XLA Ops:
  1.3 1.3 %select_reduce_fusion.slots = s32[64]{0:T(128)} fusion(s32[24]{0:T(128)} %bitcast.9, pred[24]{0:T(512)(128)(4,1)S(1)} %iota_compare_fusion.1), kind=kLoop, calls=%fused_computation | loop fusion | flops 6080 | bytes 376 | tf_op jit(solution)/shard_map/reduce_min | solution.py:563
  2.5 106.1 %graph_layer.1 = (bf16[256,256]{1,0:T(8,128)(2,1)}, bf16[256,256]{1,0:T(8,128)(2,1)}, f32[256,256]{1,0:T(8,128)}, f32[8,256]{1,0:T(8,128)}) custom-call(s32[64]{0:T(128)} %select_reduce_fusion.slots, bf16[256,256]{1,0:T(8,128)(2,1)} %features.1, bf16[256,256]{1,0:T(8,128)(2,1)} %weight.1, f32[1,256]{1,0:T(1,128)} %bitcast.8, bf16[24,512,512]{2,1,0:T(8,128)(2,1)} %bitcast.6, ...), custom_call_target="tpu_custom_call" | custom-call | tf_op jit(solution)/shard_map/graph_layer/pallas_call | solution.py:566
  108.6 1.3 %slice.3 = f32[1,256]{1,0:T(1,128)} slice(f32[8,256]{1,0:T(8,128)} %get-tuple-element.11), slice={[0:1], [0:256]} | slice | bytes 2048 | tf_op jit(solution)/shard_map/slice | solution.py:622
  109.9 1.6 %copy.15 = bf16[256,256]{1,0:T(8,128)(2,1)} copy(bf16[256,256]{1,0:T(8,128)(2,1)} %get-tuple-element.16) | data formatting | bytes 262144
  111.4 1.6 %copy.16 = bf16[256,256]{1,0:T(8,128)(2,1)} copy(bf16[256,256]{1,0:T(8,128)(2,1)} %get-tuple-element.17) | data formatting | bytes 262144
  113.0 1.7 %copy.17 = f32[256,256]{1,0:T(8,128)} copy(f32[256,256]{1,0:T(8,128)} %get-tuple-element.18) | data formatting | bytes 524288
  (1 shorter events, 0.0 us)

commit v2 on v1

v2 whole, which is shorter than its diff:
```python
import math

import jax
import jax.numpy as jnp
from jax import lax
from jax.experimental import pallas as pl
from jax.experimental.pallas import tpu as pltpu
from jax.sharding import PartitionSpec as P

MESH = pl.DeviceIdType.MESH
F32 = jnp.float32
BF16 = jnp.bfloat16
N = 256
HALF = 128
TILE = 512
SLOTS = 24
LOADS = 8
LAG = 2
EARLY = 4
GAP = 3
HA = 2
HB = 5
HC = 9
HD = 13
HE = 17
RV = 3
CV = 6


def pick(index, options):
    value = options[-1]
    for place in range(len(options) - 2, -1, -1):
        value = jnp.where(index == place, options[place], value)
    return value


def order_far_first(j, z):
    low = jnp.where(z < 2, z, 3 - z)
    base = jnp.where(low == 0, 3 - j, pick(j, [3, 0, 2, 1]))
    return jnp.where(z < 2, base, 3 - base)


def order_near_first(j, z):
    low = jnp.where(z < 2, z, 3 - z)
    base = jnp.where(low == 0, j, pick(j, [1, 0, 2, 3]))
    return jnp.where(z < 2, base, 3 - base)


def split_dot(left, right, dims):
    high = left.astype(BF16)
    low = (left - high.astype(F32)).astype(BF16)
    return lax.dot_general(high, right, dims, preferred_element_type=F32) + lax.dot_general(
        low, right, dims, preferred_element_type=F32
    )


def kernel(
    slots, features, weight, bias, tiles_hbm, cotangent,
    output, grad_features, grad_weight, grad_bias,
    tiles, feat, pair_out, pair_in, xa, xb, xc, xra, xrb, xrc, zs, zr,
    sig, acc, ya, yb, yc, yra, yrb, yrc, qs, qr,
    wa, wra, wb, wk, wc, wx, wz, wd, we, wg, work, part_sums,
    weight_in, bias_in, cotangent_in, output_out, features_out, weight_out, bias_out,
    load_sem, fy_s, fy_r, fh_s, fh_r, pair_s, pair_r, x_s, x_r, z_s, z_r,
    gp_s, gp_r, gx_s, gx_r, gz_s, gz_r, y_s, y_r, q_s, q_r,
    wa_s, wa_r, wk_s, wk_r, wx_s, wx_r, wz_s, wz_r, wd_s, wd_r, we_s, we_r, wg_s, wg_r, in_sem, out_sem,
):
    row, col = lax.axis_index("row"), lax.axis_index("col")
    y, h = row // 2, row % 2
    x, z, k = col // 8, (col // 2) % 4, col % 2
    other = 1 - k
    scale = 1.0 / math.sqrt(65536)

    def column(xx, zz, kk):
        return (xx * 4 + zz) * 2 + kk

    def remote(src, dst, send, recv, to_row, to_col):
        return pltpu.make_async_remote_copy(
            src_ref=src, dst_ref=dst, send_sem=send, recv_sem=recv,
            device_id=(to_row, to_col), device_id_type=MESH,
        )

    x_next = [column((x + 1) % 4, z, k), column((x + 3) % 4, z, k)]
    y_next = [((y + 1) % 4) * 2 + h, ((y + 3) % 4) * 2 + h]
    z_up = column(x, jnp.minimum(z + 1, 3), k)
    z_down = column(x, jnp.maximum(z - 1, 0), k)
    z_next = [z_up, z_down]
    twin = column(x, z, other)
    across = y * 2 + 1 - h
    edge = (z == 0) | (z == 3)

    def rows(half):
        return pl.ds(half * HALF, HALF)

    barrier = pltpu.get_barrier_semaphore()
    partners = [(row, twin)]
    for step in range(1, 4):
        partners.append((row, column((x + step) % 4, z, k)))
        partners.append((((y + step) % 4) * 2 + h, col))
    for step in range(1, 8):
        place = (h * 4 + z + step) % 8
        partners.append((y * 2 + place // 4, column(x, place % 4, k)))
    for to_row, to_col in partners:
        pl.semaphore_signal(barrier, inc=1, device_id=(to_row, to_col), device_id_type=MESH)

    def tile_load(part):
        count = SLOTS // LOADS
        return pltpu.make_async_copy(
            tiles_hbm.at[pl.ds(part * count, count)], tiles.at[pl.ds(part * count, count)], load_sem.at[part]
        )

    def load(part):
        src, dst = ((weight, weight_in), (bias, bias_in), (cotangent, cotangent_in))[part]
        return pltpu.make_async_copy(src, dst, in_sem.at[part])

    def output_store():
        return pltpu.make_async_copy(output_out, output, out_sem.at[0])

    def features_store():
        return pltpu.make_async_copy(features_out, grad_features, out_sem.at[1])

    def weight_store():
        return pltpu.make_async_copy(weight_out, grad_weight, out_sem.at[2])

    def bias_store():
        return pltpu.make_async_copy(bias_out, grad_bias, out_sem.at[3])

    mine = pltpu.make_async_copy(features, feat.at[pl.ds(row * N, N)], in_sem.at[3])
    mine.start()
    for part in range(LOADS):
        tile_load(part).start()
    for part in range(3):
        load(part).start()
    mine.wait()
    pl.semaphore_wait(barrier, len(partners))

    def feat_rows(yy, hh, half):
        return feat.at[pl.ds((yy * 2 + hh) * N + half * HALF, HALF)]

    def feat_across(half):
        here = feat_rows(y, h, half)
        return remote(here, here, fh_s.at[half], fh_r.at[half], across, col)

    def feat_across_in(half):
        there = feat_rows(y, 1 - h, half)
        return remote(there, there, fh_s.at[half], fh_r.at[half], across, col)

    def feat_y(kind, way, g):
        hh = h if g == 0 else 1 - h
        behind = (y + (3 if way == 0 else 1)) % 4
        block = feat_rows(behind if kind == 2 else y, hh, way if kind != 1 else 1 - way)
        return remote(block, block, fy_s.at[kind, way, g], fy_r.at[kind, way, g], y_next[way], col)

    def feat_y_in(kind, way, g):
        hh = h if g == 0 else 1 - h
        behind = (y + (3 if way == 0 else 1)) % 4
        source = (y + 2) % 4 if kind == 2 else behind
        block = feat_rows(source, hh, way if kind != 1 else 1 - way)
        return remote(block, block, fy_s.at[kind, way, g], fy_r.at[kind, way, g], y_next[way], col)

    for half in range(2):
        feat_across(half).start()
    for way in range(2):
        feat_y(0, way, 0).start()
    tiles[SLOTS] = jnp.zeros((TILE, TILE), BF16)
    acc[...] = jnp.zeros(acc.shape, F32)
    for way in range(2):
        feat_y(0, way, 0).wait_send()
    for way in range(2):
        feat_y(1, way, 0).start()
    for way in range(2):
        feat_y_in(0, way, 0).wait_recv()
        feat_y(2, way, 0).start()
    for way in range(2):
        feat_y_in(1, way, 0).wait_recv()
        feat_y_in(2, way, 0).wait_recv()
    for part in range(LOADS):
        tile_load(part).wait()

    def row_tile(s):
        xx = (x + pick(s % 4, [2, 1, 3, 0])) % 4
        return xx * 4 + order_far_first(s // 4, z)

    def forward_half(t, k_half, hh):
        total = None
        lanes = pl.ds(pl.multiple_of(hh * N, N), N)
        for c in range(4):
            part = jnp.dot(
                tiles[slots[t * 4 + c], pl.ds(pl.multiple_of(k_half * N, N), N), lanes],
                feat[pl.ds(pl.multiple_of((c * 2 + hh) * N, N), N), :],
                preferred_element_type=F32,
            )
            total = part if total is None else total + part
        return total

    def early_step(s, carry):
        @pl.when(s == EARLY)
        def _():
            for half in range(2):
                feat_across_in(half).wait_recv()
                feat_y(0, half, 1).start()

        @pl.when(s == EARLY + GAP)
        def _():
            for way in range(2):
                feat_y(1, way, 1).start()

        @pl.when(s == EARLY + GAP + 2)
        def _():
            for way in range(2):
                feat_y_in(0, way, 1).wait_recv()
                feat_y(2, way, 1).start()

        t = row_tile(s)
        part_sums[s, 0] = forward_half(t, other, h)
        part_sums[s, 1] = forward_half(t, k, h)
        return carry

    lax.fori_loop(0, 16, early_step, 0)
    for way in range(2):
        feat_y_in(1, way, 1).wait_recv()
        feat_y_in(2, way, 1).wait_recv()

    def pair_copy(u):
        return remote(pair_out.at[u], pair_in.at[u], pair_s.at[u], pair_r.at[u], row, twin)

    def x_copy(kind, way, j):
        if kind == 0:
            src, dst = xa.at[j, rows(way)], xra.at[way, j]
        elif kind == 1:
            src, dst = xb.at[way, j], xrb.at[way, j]
        else:
            src, dst = xc.at[way, j], xrc.at[way, j]
        return remote(src, dst, x_s.at[kind, way, j], x_r.at[kind, way, j], row, x_next[way])

    def z_copy(j):
        target = order_far_first(j, z)
        way = jnp.where(target > z, 0, 1)
        to = jnp.where(target > z, z_up, z_down)
        return remote(zs.at[j], zr.at[way, target], z_s.at[j], z_r.at[way, target], row, to)

    def z_wait(way, target):
        block = zr.at[way, target]
        remote(zs.at[0], block, z_s.at[0], z_r.at[way, target], row, twin).wait_recv()

    def relay(j):
        for way in range(2):
            x_copy(0, way, j).wait_recv()
            xc[way, j] = (part_sums[4 * j + 1 + way, 1, rows(way), :] + xra[way, j].astype(F32)).astype(BF16)
            x_copy(2, way, j).start()

    def collect(j):
        u = 4 * j + 3
        for way in range(2):
            x_copy(1, way, j).wait_recv()
            x_copy(2, way, j).wait_recv()
        for half in range(2):
            part_sums[u, 1, rows(half), :] = (
                part_sums[u, 1, rows(half), :] + xrc[half, j].astype(F32) + xrb[1 - half, j].astype(F32)
            )

        @pl.when(edge & (j < 3))
        def _():
            zs[j] = part_sums[u, 1].astype(BF16)
            z_copy(j).start()

        def middle(jj):
            target = order_far_first(jj, z)
            way = jnp.where(target > z, 0, 1)
            z_wait(way, target)
            zs[jj] = (part_sums[4 * jj + 3, 1] + zr[way, target].astype(F32)).astype(BF16)
            z_copy(jj).start()

        @pl.when(jnp.logical_not(edge) & (j == 1))
        def _():
            middle(0)

        @pl.when(jnp.logical_not(edge) & (j == 2))
        def _():
            middle(1)
            middle(2)

    def forward_step(s, carry):
        @pl.when(s < 16)
        def _():
            t = row_tile(s)
            pair_out[s] = (part_sums[s, 0] + forward_half(t, other, 1 - h)).astype(BF16)
            pair_copy(s).start()
            part_sums[s, 1] = part_sums[s, 1] + forward_half(t, k, 1 - h)

        @pl.when((s >= LAG) & (s < 16 + LAG))
        def _():
            u = s - LAG
            j = u // 4
            pair_copy(u).wait_recv()

            @pl.when(u % 4 == 0)
            def _():
                xa[j] = (part_sums[u, 1] + pair_in[u].astype(F32)).astype(BF16)
                x_copy(0, 0, j).start()
                x_copy(0, 1, j).start()

            for way in range(2):

                @pl.when(u % 4 == 1 + way)
                def _():
                    far, near = rows(way), rows(1 - way)
                    xb[way, j] = (part_sums[u, 1, near, :] + pair_in[u, near, :].astype(F32)).astype(BF16)
                    x_copy(1, way, j).start()
                    part_sums[u, 1, far, :] = part_sums[u, 1, far, :] + pair_in[u, far, :].astype(F32)

            @pl.when(u % 4 == 3)
            def _():
                part_sums[u, 1] = part_sums[u, 1] + pair_in[u].astype(F32)

        v = s - LAG - RV

        @pl.when((v >= 0) & (v < 16) & (v % 4 == 0))
        def _():
            relay(v // 4)

        w = s - LAG - CV

        @pl.when((w >= 0) & (w % 4 == 0))
        def _():
            collect(w // 4)

        return carry

    lax.fori_loop(0, LAG + CV + 13, forward_step, 0)

    @pl.when(z > 0)
    def _():
        z_wait(0, z)
        part_sums[15, 1] = part_sums[15, 1] + zr[0, z].astype(F32)

    @pl.when(z < 3)
    def _():
        z_wait(1, z)
        part_sums[15, 1] = part_sums[15, 1] + zr[1, z].astype(F32)

    gathered = part_sums[15, 1]
    for part in range(3):
        load(part).wait()
    shifted = split_dot(gathered, weight_in[...], (((1,), (0,)), ((), ()))) + bias_in[...]
    sigma = jax.nn.sigmoid(shifted)
    output_out[...] = (shifted * sigma).astype(BF16)
    output_store().start()
    signal = (cotangent_in[...].astype(F32) * (sigma * (1.0 + shifted * (1.0 - sigma)))).astype(BF16)
    work[...] = signal
    sig[x * 4 + z, k] = signal.astype(F32).T.astype(BF16)

    def sig_pair(t, kk):
        block = sig.at[t, kk]
        return remote(block, block, gp_s.at[t], gp_r.at[t], row, twin)

    def sig_z(way, piece):
        block = sig.at[x * 4 + piece, k]
        return remote(block, block, gz_s.at[way, piece], gz_r.at[way, piece], row, z_next[way])

    def sig_x(kind, way, j, arriving=False):
        piece = order_near_first(j, z)
        behind = (x + (3 if way == 0 else 1)) % 4
        if arriving:
            source = (x + 2) % 4 if kind == 2 else behind
        else:
            source = behind if kind == 2 else x
        block = sig.at[source * 4 + piece, k, rows(way if kind != 1 else 1 - way)]
        return remote(block, block, gx_s.at[kind, way, j], gx_r.at[kind, way, j], row, x_next[way])

    def launch_piece(j):
        for kind in range(2):
            for way in range(2):
                sig_x(kind, way, j).start()
        sig_pair(x * 4 + order_near_first(j, z), k).start()

    for way in range(2):
        sig_x(0, way, 0).start()

    @pl.when(z < 3)
    def _():
        sig_z(0, z).start()

    @pl.when(z > 0)
    def _():
        sig_z(1, z).start()

    sig_pair(x * 4 + z, k).start()

    def wa_copy(to, here):
        return remote(wa.at[to], wra.at[here], wa_s.at[to], wa_r.at[here], to * 2 + h, col)

    def wk_copy():
        return remote(wb.at[other], wk, wk_s.at[0], wk_r.at[0], row, twin)

    def wx_copy(to, here):
        return remote(wc.at[to], wx.at[here], wx_s.at[to], wx_r.at[here], row, column(to, z, k))

    def wz_copy(to, here):
        return remote(
            wz.at[here], wz.at[here], wz_s.at[to], wz_r.at[here], y * 2 + to // 4, column(x, to % 4, k)
        )

    def wd_copy(to, here):
        return remote(wd.at[here], wd.at[here], wd_s.at[to], wd_r.at[here], row, column(to, z, k))

    def we_copy(here):
        return remote(we.at[here], we.at[here], we_s.at[0], we_r.at[0], row, twin)

    def wg_copy(to, here):
        return remote(wg.at[here], wg.at[here], wg_s.at[to], wg_r.at[here], to * 2 + h, col)

    def total_of(ref, count):
        total = ref[0]
        for place in range(1, count):
            total = total + ref[place]
        return total

    place8 = h * 4 + z

    part = split_dot(gathered.T, work[...], (((1,), (0,)), ((), ())))
    bias_part = jnp.sum(work[...].astype(F32), axis=0, keepdims=True)
    line = lax.broadcasted_iota(jnp.int32, (8, HALF), 0)
    bias_block = jnp.where(line == 0, jnp.broadcast_to(bias_part[:, 0:HALF], (8, HALF)), 0.0) + jnp.where(
        line == 1, jnp.broadcast_to(bias_part[:, HALF:N], (8, HALF)), 0.0
    )
    for piece in range(32):
        wa[piece // 8, piece // 4 % 2, piece % 4, :, 0:N] = part[piece * 8 : piece * 8 + 8, :]
        wa[piece // 8, piece // 4 % 2, piece % 4, :, N : N + HALF] = bias_block
    for way in range(2):
        sig_x(1, way, 0).start()
    for step in range(1, 4):
        wa_copy((y + step) % 4, y).start()
    wra[y] = wa[y]

    def weights_rows():
        for step in range(1, 4):
            wa_copy((y + step) % 4, (y + step) % 4).wait_recv()
        wb[...] = total_of(wra, 4)
        wk_copy().start()

    def weights_pair():
        wk_copy().wait_recv()
        wc[...] = wb[k] + wk[...]
        for step in range(1, 4):
            wx_copy((x + step) % 4, x).start()
        wx[x] = wc[x]

    def weights_x():
        for step in range(1, 4):
            wx_copy((x + step) % 4, (x + step) % 4).wait_recv()
        wz[place8] = total_of(wx, 4)
        for step in range(1, 8):
            wz_copy((place8 + step) % 8, place8).start()

    def weights_z():
        for step in range(1, 8):
            wz_copy((place8 + step) % 8, (place8 + step) % 8).wait_recv()
        wd[x] = total_of(wz, 8) * scale
        for step in range(1, 4):
            wd_copy((x + step) % 4, x).start()

    def weights_back():
        for step in range(1, 4):
            wd_copy((x + step) % 4, (x + step) % 4).wait_recv()
        we[k] = wd[...]
        we_copy(k).start()

    def weights_twin():
        we_copy(other).wait_recv()
        wg[y] = we[...]
        for step in range(1, 4):
            wg_copy((y + step) % 4, y).start()

    def weights_end():
        for step in range(1, 4):
            wg_copy((y + step) % 4, (y + step) % 4).wait_recv()
        for piece in range(32):
            weight_out[piece * 8 : piece * 8 + 8, :] = wg[piece // 8, piece // 4 % 2, piece % 4, :, 0:N]
        bias_out[0:1, 0:HALF] = wg[0, 0, 0, 0:1, N : N + HALF]
        bias_out[0:1, HALF:N] = wg[0, 0, 0, 1:2, N : N + HALF]
        weight_store().start()
        bias_store().start()

    def relay_signal(j):
        for way in range(2):
            sig_x(0, way, j, True).wait_recv()
            sig_x(2, way, j).start()

    def next_piece(jj):
        piece = order_near_first(jj, z)

        @pl.when(z == 0)
        def _():
            sig_z(1, piece).wait_recv()

        @pl.when(z == 3)
        def _():
            sig_z(0, piece).wait_recv()

        @pl.when(jnp.logical_not(edge) & (jj == 1))
        def _():
            sig_z(0, z - 1).wait_recv()
            sig_z(0, z - 1).start()
            sig_z(1, z + 1).wait_recv()
            sig_z(1, z + 1).start()

        @pl.when((z == 1) & (jj == 2))
        def _():
            sig_z(1, 3).wait_recv()
            sig_z(1, 3).start()

        @pl.when((z == 2) & (jj == 2))
        def _():
            sig_z(0, 0).wait_recv()
            sig_z(0, 0).start()

        launch_piece(jj)

    def backward_step(s, carry):
        j = s // 4

        @pl.when(s == 0)
        def _():
            relay_signal(0)
            next_piece(1)

        @pl.when((s == 4) | (s == 8))
        def _():
            next_piece(j + 1)

        @pl.when((s % 4 == 0) & (s >= 4) & (s < 16))
        def _():
            relay_signal(j)

        @pl.when((s % 4 == 0) & (s >= 4))
        def _():
            for way in range(2):
                sig_x(2, way, j - 1, True).wait_recv()
            sig_pair(((x + 2) % 4) * 4 + order_near_first(j - 1, z), k).start()

        @pl.when((s % 4 == 1) & (s < 16))
        def _():
            piece = order_near_first(j, z)
            for way in range(2):
                sig_x(1, way, j, True).wait_recv()
                sig_pair(((x + (3 if way == 0 else 1)) % 4) * 4 + piece, k).start()

        for when, what in (
            (HA, weights_rows), (HB, weights_pair), (HC, weights_x), (HD, weights_z), (HE, weights_back),
        ):

            @pl.when(s == when)
            def _(what=what):
                what()

        last = s % 4 == 1

        @pl.when((s != 1) & (s != 16))
        def _():
            jj = jnp.where(last, j - 1, j)
            shift = pick(s % 4, [0, 2, 3, 1])
            t = ((x + shift) % 4) * 4 + order_near_first(jj, z)
            sig_pair(t, other).wait_recv()
            for c in range(4):
                slot = slots[t * 4 + c]
                part = jnp.dot(sig[t, 0], tiles[slot, 0:N, :], preferred_element_type=F32) + jnp.dot(
                    sig[t, 1], tiles[slot, N:TILE, :], preferred_element_type=F32
                )
                acc[c, 0] += part[:, 0:N]
                acc[c, 1] += part[:, N:TILE]

        return carry

    lax.fori_loop(0, 18, backward_step, 0)

    def y_copy(kind, way, g):
        if kind == 0:
            src, dst = ya.at[g, rows(way)], yra.at[way, g]
        elif kind == 1:
            src, dst = yb.at[way, g], yrb.at[way, g]
        else:
            src, dst = yc.at[way, g], yrc.at[way, g]
        return remote(src, dst, y_s.at[kind, way, g], y_r.at[kind, way, g], y_next[way], col)

    def y_open(g):
        hh = 1 - h if g == 0 else h
        ya[g] = acc[(y + 2) % 4, hh].astype(BF16)
        for way in range(2):
            y_copy(0, way, g).start()
        if g == 0:
            for way in range(2):
                y_copy(0, way, 0).wait_send()
        for way in range(2):
            yb[way, g] = acc[(y + (1 if way == 0 else 3)) % 4, hh, rows(1 - way), :].astype(BF16)
            y_copy(1, way, g).start()

    def y_relay(g):
        hh = 1 - h if g == 0 else h
        for way in range(2):
            y_copy(0, way, g).wait_recv()
            near = acc[(y + (1 if way == 0 else 3)) % 4, hh, rows(way), :]
            yc[way, g] = (near + yra[way, g].astype(F32)).astype(BF16)
            y_copy(2, way, g).start()

    def y_close(g):
        hh = 1 - h if g == 0 else h
        for way in range(2):
            y_copy(1, way, g).wait_recv()
            y_copy(2, way, g).wait_recv()
        for half in range(2):
            acc[y, hh, rows(half), :] = (
                acc[y, hh, rows(half), :] + yrc[half, g].astype(F32) + yrb[1 - half, g].astype(F32)
            )

    def q_copy(half):
        return remote(qs.at[half], qr.at[half], q_s.at[half], q_r.at[half], across, col)

    y_open(0)
    y_relay(0)
    for way in range(2):
        y_copy(2, way, 0).wait_send()
    y_open(1)
    weights_twin()
    y_close(0)
    for half in range(2):
        qs[half] = acc[y, 1 - h, rows(half), :].astype(BF16)
        q_copy(half).start()
    y_relay(1)
    y_close(1)
    weights_end()
    for half in range(2):
        q_copy(half).wait_recv()
        acc[y, h, rows(half), :] = acc[y, h, rows(half), :] + qr[half].astype(F32)
    features_out[...] = split_dot(acc[y, h].T, weight_in[...], (((1,), (1,)), ((), ()))).astype(BF16)
    features_store().start()


    for half in range(2):
        feat_across(half).wait_send()
        q_copy(half).wait_send()
    for kind in range(3):
        for way in range(2):
            for g in range(2):
                if (kind, g) != (0, 0):
                    feat_y(kind, way, g).wait_send()
                if g == 1 or kind == 1:
                    y_copy(kind, way, g).wait_send()

    def sent_pair(u, carry):
        pair_copy(u).wait_send()
        sig_pair(u, k).wait_send()
        return carry

    lax.fori_loop(0, 16, sent_pair, 0)

    def sent_x(j, carry):
        for kind in range(3):
            for way in range(2):
                x_copy(kind, way, j).wait_send()
                sig_x(kind, way, j).wait_send()
        return carry

    lax.fori_loop(0, 4, sent_x, 0)
    for j in range(3):
        z_copy(j).wait_send()
    for piece in range(4):

        @pl.when((z < 3) & (piece <= z))
        def _():
            sig_z(0, piece).wait_send()

        @pl.when((z > 0) & (piece >= z))
        def _():
            sig_z(1, piece).wait_send()

    for step in range(1, 4):
        wa_copy((y + step) % 4, y).wait_send()
        wx_copy((x + step) % 4, x).wait_send()
        wd_copy((x + step) % 4, x).wait_send()
        wg_copy((y + step) % 4, y).wait_send()
    for step in range(1, 8):
        wz_copy((place8 + step) % 8, place8).wait_send()
    wk_copy().wait_send()
    we_copy(k).wait_send()
    output_store().wait()
    weight_store().wait()
    bias_store().wait()
    features_store().wait()


def hand_over(output, grad_features, grad_weight, grad_bias, output_to, features_to, weight_to, bias_to):
    output_to[...] = output[...]
    features_to[...] = grad_features[...]
    weight_to[...] = grad_weight[...]
    bias_to[...] = grad_bias[...]


def on_device(features, weight, bias_vector, adjacency_tiles, tile_index, tile_count, grad_output):
    located = tile_index[0, 0]
    places = jnp.arange(SLOTS, dtype=jnp.int32)[:, None]
    hit = (located[:, None] == jnp.arange(64, dtype=jnp.int32)[None, :]) & (places < tile_count[0, 0])
    slots = jnp.min(jnp.where(hit, places, SLOTS), axis=0)
    vmem = pl.BlockSpec(memory_space=pltpu.VMEM)
    anywhere = pl.BlockSpec(memory_space=pl.ANY)
    dma = pltpu.SemaphoreType.DMA
    output, grad_features, grad_weight, grad_bias = pl.pallas_call(
        kernel,
        out_shape=(
            jax.ShapeDtypeStruct((N, N), BF16),
            jax.ShapeDtypeStruct((N, N), BF16),
            jax.ShapeDtypeStruct((N, N), F32),
            jax.ShapeDtypeStruct((1, N), F32),
        ),
        in_specs=[
            pl.BlockSpec(memory_space=pltpu.SMEM), anywhere, anywhere, anywhere, anywhere, anywhere,
        ],
        out_specs=(anywhere, anywhere, anywhere, anywhere),
        scratch_shapes=[
            pltpu.VMEM((SLOTS + 1, TILE, TILE), BF16),
            pltpu.VMEM((8 * N, N), BF16),
            pltpu.VMEM((16, N, N), BF16),
            pltpu.VMEM((16, N, N), BF16),
            pltpu.VMEM((4, N, N), BF16),
            pltpu.VMEM((2, 4, HALF, N), BF16),
            pltpu.VMEM((2, 4, HALF, N), BF16),
            pltpu.VMEM((2, 4, HALF, N), BF16),
            pltpu.VMEM((2, 4, HALF, N), BF16),
            pltpu.VMEM((2, 4, HALF, N), BF16),
            pltpu.VMEM((3, N, N), BF16),
            pltpu.VMEM((2, 4, N, N), BF16),
            pltpu.VMEM((16, 2, N, N), BF16),
            pltpu.VMEM((4, 2, N, N), F32),
            pltpu.VMEM((2, N, N), BF16),
            pltpu.VMEM((2, 2, HALF, N), BF16),
            pltpu.VMEM((2, 2, HALF, N), BF16),
            pltpu.VMEM((2, 2, HALF, N), BF16),
            pltpu.VMEM((2, 2, HALF, N), BF16),
            pltpu.VMEM((2, 2, HALF, N), BF16),
            pltpu.VMEM((2, HALF, N), BF16),
            pltpu.VMEM((2, HALF, N), BF16),
            pltpu.VMEM((4, 2, 4, 8, N + HALF), F32),
            pltpu.VMEM((4, 2, 4, 8, N + HALF), F32),
            pltpu.VMEM((2, 4, 8, N + HALF), F32),
            pltpu.VMEM((4, 8, N + HALF), F32),
            pltpu.VMEM((4, 8, N + HALF), F32),
            pltpu.VMEM((4, 8, N + HALF), F32),
            pltpu.VMEM((8, 8, N + HALF), F32),
            pltpu.VMEM((4, 8, N + HALF), F32),
            pltpu.VMEM((2, 4, 8, N + HALF), F32),
            pltpu.VMEM((4, 2, 4, 8, N + HALF), F32),
            pltpu.VMEM((N, N), BF16),
            pltpu.VMEM((16, 2, N, N), F32),
            pltpu.VMEM((N, N), BF16),
            pltpu.VMEM((1, N), F32),
            pltpu.VMEM((N, N), BF16),
            pltpu.VMEM((N, N), BF16),
            pltpu.VMEM((N, N), BF16),
            pltpu.VMEM((N, N), F32),
            pltpu.VMEM((1, N), F32),
            dma((LOADS,)),
            dma((3, 2, 2)), dma((3, 2, 2)), dma((2,)), dma((2,)),
            dma((16,)), dma((16,)), dma((3, 2, 4)), dma((3, 2, 4)), dma((3,)), dma((2, 4)),
            dma((16,)), dma((16,)), dma((3, 2, 4)), dma((3, 2, 4)), dma((2, 4)), dma((2, 4)),
            dma((3, 2, 2)), dma((3, 2, 2)), dma((2,)), dma((2,)),
            dma((4,)), dma((4,)), dma((1,)), dma((1,)), dma((4,)), dma((4,)), dma((8,)), dma((8,)),
            dma((4,)), dma((4,)), dma((1,)), dma((1,)), dma((4,)), dma((4,)), dma((4,)), dma((4,)),
        ],
        compiler_params=pltpu.CompilerParams(
            collective_id=0, has_side_effects=True, vmem_limit_bytes=56 * 1024 * 1024
        ),
        name="graph_layer",
    )(slots, features, weight, bias_vector[None, :], adjacency_tiles[0, 0], grad_output)
    output, grad_features, grad_weight, grad_bias = pl.pallas_call(
        hand_over,
        out_shape=(
            jax.ShapeDtypeStruct((N, N), BF16),
            jax.ShapeDtypeStruct((N, N), BF16),
            jax.ShapeDtypeStruct((N, N), F32),
            jax.ShapeDtypeStruct((1, N), F32),
        ),
        in_specs=[vmem, vmem, vmem, vmem],
        out_specs=(vmem, vmem, vmem, vmem),
        name="hand_over",
    )(output, grad_features, grad_weight, grad_bias)
    return output, grad_features, grad_weight, grad_bias[0]


def solution(mesh):
    return jax.shard_map(
        on_device,
        mesh=mesh,
        in_specs=(
            P(("col", "row"), None),
            P(),
            P(),
            P("row", "col", None, None, None),
            P("row", "col", None),
            P("row", "col"),
            P(("row", "col"), None),
        ),
        out_specs=(P(("row", "col"), None), P(("col", "row"), None), P(), P()),
        check_vma=False,
    )
```

time: 117 us -> 105 us (0.90)
  local copies, waits for them, and re-layouts: 6.06 us -> 0 us
  Pallas kernels: 106 us -> 101 us
    pallas_call x1, Pallas kernels: 106 us -> 99.2 us  [on_device(): pl.pallas_call(kernel, out_shape=(jax.ShapeDtypeStruct((N, N), BF16), jax...]
    unnamed x3 -> x0, local copies, waits for them, and re-layouts: 4.8 us -> none
    pallas_call x0 -> x1, Pallas kernels: none -> 1.89 us  [on_device(): pl.pallas_call(hand_over, out_shape=(jax.ShapeDtypeStruct((N, N), BF16),...]
    slice x1 -> x0, local copies, waits for them, and re-layouts: 1.26 us -> none  [on_device(): return (output, grad_features, grad_weight, grad_bias[0])]
where the time goes in v2:
time: 105 us; the launch traced here: 104 us
  Pallas kernels  101 us (96%)
  between operations  1.29 us (1%)
  other arithmetic  1.26 us (1%)
    pallas_call x1, Pallas kernels, on_device(): pl.pallas_call(kernel, out_shape=(jax.ShapeDtypeStruct((N, N), BF16), jax...  99.2 us

profile of v2, /device:TPU:8, one launch (start us, length us, event | category | flops | bytes accessed | tf_op | source)
XLA Modules:
  0.0 103.6 jit_solution(2815661181377450164)
XLA Ops:
  1.3 1.3 %select_reduce_fusion.slots = s32[64]{0:T(128)} fusion(s32[24]{0:T(128)} %bitcast.9, pred[24]{0:T(512)(128)(4,1)S(1)} %iota_compare_fusion.1), kind=kLoop, calls=%fused_computation | loop fusion | flops 6080 | bytes 376 | tf_op jit(solution)/shard_map/reduce_min | solution.py:703
  2.5 99.2 %graph_layer.1 = (bf16[256,256]{1,0:T(8,128)(2,1)}, bf16[256,256]{1,0:T(8,128)(2,1)}, f32[256,256]{1,0:T(8,128)}, f32[1,256]{1,0:T(1,128)}) custom-call(s32[64]{0:T(128)} %select_reduce_fusion.slots, bf16[256,256]{1,0:T(8,128)(2,1)} %features.1, bf16[256,256]{1,0:T(8,128)(2,1)} %weight.1, f32[1,256]{1,0:T(1,128)} %bitcast.7, bf16[24,512,512]{2,1,0:T(8,128)(2,1)} %bitcast.6, ...), custom_call_target="tpu_custom_call" | custom-call | tf_op jit(solution)/shard_map/graph_layer/pallas_call | solution.py:707
  101.7 1.9 %hand_over.1 = (bf16[256,256]{1,0:T(8,128)(2,1)}, bf16[256,256]{1,0:T(8,128)(2,1)}, f32[256,256]{1,0:T(8,128)}, f32[1,256]{1,0:T(1,128)}) custom-call(bf16[256,256]{1,0:T(8,128)(2,1)} %get-tuple-element.12.output, bf16[256,256]{1,0:T(8,128)(2,1)} %get-tuple-element.13.grad_features, f32[256,256]{1,0:T(8,128)} %get-tuple-element.14.grad_weight, ...), custom_call_target="tpu_custom_call" | custom-call | tf_op jit(solution)/shard_map/hand_over/pallas_call | solution.py:774
  (1 shorter events, 0.0 us)

commit v3 on v2

--- a/solution.py
+++ b/solution.py
@@ -55,7 +55,7 @@
 
 
 def kernel(
-    slots, features, weight, bias, tiles_hbm, cotangent,
+    located, limit, features, weight, bias, tiles_hbm, cotangent,
     output, grad_features, grad_weight, grad_bias,
     tiles, feat, pair_out, pair_in, xa, xb, xc, xra, xrb, xrc, zs, zr,
     sig, acc, ya, yb, yc, yra, yrb, yrc, qs, qr,
@@ -63,7 +63,7 @@
     weight_in, bias_in, cotangent_in, output_out, features_out, weight_out, bias_out,
     load_sem, fy_s, fy_r, fh_s, fh_r, pair_s, pair_r, x_s, x_r, z_s, z_r,
     gp_s, gp_r, gx_s, gx_r, gz_s, gz_r, y_s, y_r, q_s, q_r,
-    wa_s, wa_r, wk_s, wk_r, wx_s, wx_r, wz_s, wz_r, wd_s, wd_r, we_s, we_r, wg_s, wg_r, in_sem, out_sem,
+    wa_s, wa_r, wk_s, wk_r, wx_s, wx_r, wz_s, wz_r, wd_s, wd_r, we_s, we_r, wg_s, wg_r, in_sem, out_sem, slots,
 ):
     row, col = lax.axis_index("row"), lax.axis_index("col")
     y, h = row // 2, row % 2
@@ -171,6 +171,15 @@
     for way in range(2):
         feat_y_in(0, way, 0).wait_recv()
         feat_y(2, way, 0).start()
+
+    def fill(place, carry):
+        slot = SLOTS
+        for i in range(SLOTS):
+            slot = jnp.where((located[i] == place) & (limit[0] > i), i, slot)
+        slots[place] = slot
+        return carry
+
+    lax.fori_loop(0, 64, fill, 0)
     for way in range(2):
         feat_y_in(1, way, 0).wait_recv()
         feat_y_in(2, way, 0).wait_recv()
@@ -369,9 +378,8 @@
         return remote(block, block, gx_s.at[kind, way, j], gx_r.at[kind, way, j], row, x_next[way])
 
     def launch_piece(j):
-        for kind in range(2):
-            for way in range(2):
-                sig_x(kind, way, j).start()
+        for way in range(2):
+            sig_x(0, way, j).start()
         sig_pair(x * 4 + order_near_first(j, z), k).start()
 
     for way in range(2):
@@ -456,7 +464,11 @@
     def weights_z():
         for step in range(1, 8):
             wz_copy((place8 + step) % 8, (place8 + step) % 8).wait_recv()
-        wd[x] = total_of(wz, 8) * scale
+        total = total_of(wz, 8) * scale
+        wd[x] = total[:, 0:N]
+        bias_out[0:1, 0:HALF] = total[0:1, N : N + HALF]
+        bias_out[0:1, HALF:N] = total[1:2, N : N + HALF]
+        bias_store().start()
         for step in range(1, 4):
             wd_copy((x + step) % 4, x).start()
 
@@ -476,11 +488,8 @@
         for step in range(1, 4):
             wg_copy((y + step) % 4, (y + step) % 4).wait_recv()
         for piece in range(32):
-            weight_out[piece * 8 : piece * 8 + 8, :] = wg[piece // 8, piece // 4 % 2, piece % 4, :, 0:N]
-        bias_out[0:1, 0:HALF] = wg[0, 0, 0, 0:1, N : N + HALF]
-        bias_out[0:1, HALF:N] = wg[0, 0, 0, 1:2, N : N + HALF]
+            weight_out[piece * 8 : piece * 8 + 8, :] = wg[piece // 8, piece // 4 % 2, piece % 4]
         weight_store().start()
-        bias_store().start()
 
     def relay_signal(j):
         for way in range(2):
@@ -545,6 +554,11 @@
             for way in range(2):
                 sig_x(1, way, j, True).wait_recv()
                 sig_pair(((x + (3 if way == 0 else 1)) % 4) * 4 + piece, k).start()
+
+        @pl.when((s == 2) | (s == 6) | (s == 10))
+        def _():
+            for way in range(2):
+                sig_x(1, way, s // 4 + 1).start()
 
         for when, what in (
             (HA, weights_rows), (HB, weights_pair), (HC, weights_x), (HD, weights_z), (HE, weights_back),
@@ -588,9 +602,6 @@
         ya[g] = acc[(y + 2) % 4, hh].astype(BF16)
         for way in range(2):
             y_copy(0, way, g).start()
-        if g == 0:
-            for way in range(2):
-                y_copy(0, way, 0).wait_send()
         for way in range(2):
             yb[way, g] = acc[(y + (1 if way == 0 else 3)) % 4, hh, rows(1 - way), :].astype(BF16)
             y_copy(1, way, g).start()
@@ -616,10 +627,53 @@
     def q_copy(half):
         return remote(qs.at[half], qr.at[half], q_s.at[half], q_r.at[half], across, col)
 
+    def sent():
+        for half in range(2):
+            feat_across(half).wait_send()
+        for kind in range(3):
+            for way in range(2):
+                for g in range(2):
+                    if (kind, g) != (0, 0):
+                        feat_y(kind, way, g).wait_send()
+
+        def sent_pair(u, carry):
+            pair_copy(u).wait_send()
+            sig_pair(u, k).wait_send()
+            return carry
+
+        lax.fori_loop(0, 16, sent_pair, 0)
+
+        def sent_x(j, carry):
+            for kind in range(3):
+                for way in range(2):
+                    x_copy(kind, way, j).wait_send()
+                    sig_x(kind, way, j).wait_send()
+            return carry
+
+        lax.fori_loop(0, 4, sent_x, 0)
+        for j in range(3):
+            z_copy(j).wait_send()
+        for piece in range(4):
+
+            @pl.when((z < 3) & (piece <= z))
+            def _():
+                sig_z(0, piece).wait_send()
+
+            @pl.when((z > 0) & (piece >= z))
+            def _():
+                sig_z(1, piece).wait_send()
+
+        for step in range(1, 4):
+            wa_copy((y + step) % 4, y).wait_send()
+            wx_copy((x + step) % 4, x).wait_send()
+            wd_copy((x + step) % 4, x).wait_send()
+        for step in range(1, 8):
+            wz_copy((place8 + step) % 8, place8).wait_send()
+        wk_copy().wait_send()
+        we_copy(k).wait_send()
+
     y_open(0)
     y_relay(0)
-    for way in range(2):
-        y_copy(2, way, 0).wait_send()
     y_open(1)
     weights_twin()
     y_close(0)
@@ -629,6 +683,16 @@
     y_relay(1)
     y_close(1)
     weights_end()
+    sent()
+    for kind in range(3):
+        for way in range(2):
+            for g in range(2):
+                y_copy(kind, way, g).wait_send()
+    for step in range(1, 4):
+        wg_copy((y + step) % 4, y).wait_send()
+    output_store().wait()
+    weight_store().wait()
+    bias_store().wait()
     for half in range(2):
         q_copy(half).wait_recv()
         acc[y, h, rows(half), :] = acc[y, h, rows(half), :] + qr[half].astype(F32)
@@ -637,55 +701,7 @@
 
 
     for half in range(2):
-        feat_across(half).wait_send()
         q_copy(half).wait_send()
-    for kind in range(3):
-        for way in range(2):
-            for g in range(2):
-                if (kind, g) != (0, 0):
-                    feat_y(kind, way, g).wait_send()
-                if g == 1 or kind == 1:
-                    y_copy(kind, way, g).wait_send()
-
-    def sent_pair(u, carry):
-        pair_copy(u).wait_send()
-        sig_pair(u, k).wait_send()
-        return carry
-
-    lax.fori_loop(0, 16, sent_pair, 0)
-
-    def sent_x(j, carry):
-        for kind in range(3):
-            for way in range(2):
-                x_copy(kind, way, j).wait_send()
-                sig_x(kind, way, j).wait_send()
-        return carry
-
-    lax.fori_loop(0, 4, sent_x, 0)
-    for j in range(3):
-        z_copy(j).wait_send()
-    for piece in range(4):
-
-        @pl.when((z < 3) & (piece <= z))
-        def _():
-            sig_z(0, piece).wait_send()
-
-        @pl.when((z > 0) & (piece >= z))
-        def _():
-            sig_z(1, piece).wait_send()
-
-    for step in range(1, 4):
-        wa_copy((y + step) % 4, y).wait_send()
-        wx_copy((x + step) % 4, x).wait_send()
-        wd_copy((x + step) % 4, x).wait_send()
-        wg_copy((y + step) % 4, y).wait_send()
-    for step in range(1, 8):
-        wz_copy((place8 + step) % 8, place8).wait_send()
-    wk_copy().wait_send()
-    we_copy(k).wait_send()
-    output_store().wait()
-    weight_store().wait()
-    bias_store().wait()
     features_store().wait()
 
 
@@ -697,11 +713,8 @@
 
 
 def on_device(features, weight, bias_vector, adjacency_tiles, tile_index, tile_count, grad_output):
-    located = tile_index[0, 0]
-    places = jnp.arange(SLOTS, dtype=jnp.int32)[:, None]
-    hit = (located[:, None] == jnp.arange(64, dtype=jnp.int32)[None, :]) & (places < tile_count[0, 0])
-    slots = jnp.min(jnp.where(hit, places, SLOTS), axis=0)
     vmem = pl.BlockSpec(memory_space=pltpu.VMEM)
+    scalars = pl.BlockSpec(memory_space=pltpu.SMEM)
     anywhere = pl.BlockSpec(memory_space=pl.ANY)
     dma = pltpu.SemaphoreType.DMA
     output, grad_features, grad_weight, grad_bias = pl.pallas_call(
@@ -713,7 +726,7 @@
             jax.ShapeDtypeStruct((1, N), F32),
         ),
         in_specs=[
-            pl.BlockSpec(memory_space=pltpu.SMEM), anywhere, anywhere, anywhere, anywhere, anywhere,
+            scalars, scalars, anywhere, anywhere, anywhere, anywhere, anywhere,
         ],
         out_specs=(anywhere, anywhere, anywhere, anywhere),
         scratch_shapes=[
@@ -746,9 +759,9 @@
             pltpu.VMEM((4, 8, N + HALF), F32),
             pltpu.VMEM((4, 8, N + HALF), F32),
             pltpu.VMEM((8, 8, N + HALF), F32),
-            pltpu.VMEM((4, 8, N + HALF), F32),
-            pltpu.VMEM((2, 4, 8, N + HALF), F32),
-            pltpu.VMEM((4, 2, 4, 8, N + HALF), F32),
+            pltpu.VMEM((4, 8, N), F32),
+            pltpu.VMEM((2, 4, 8, N), F32),
+            pltpu.VMEM((4, 2, 4, 8, N), F32),
             pltpu.VMEM((N, N), BF16),
             pltpu.VMEM((16, 2, N, N), F32),
             pltpu.VMEM((N, N), BF16),
@@ -765,12 +778,13 @@
             dma((3, 2, 2)), dma((3, 2, 2)), dma((2,)), dma((2,)),
             dma((4,)), dma((4,)), dma((1,)), dma((1,)), dma((4,)), dma((4,)), dma((8,)), dma((8,)),
             dma((4,)), dma((4,)), dma((1,)), dma((1,)), dma((4,)), dma((4,)), dma((4,)), dma((4,)),
+            pltpu.SMEM((64,), jnp.int32),
         ],
         compiler_params=pltpu.CompilerParams(
             collective_id=0, has_side_effects=True, vmem_limit_bytes=56 * 1024 * 1024
         ),
         name="graph_layer",
-    )(slots, features, weight, bias_vector[None, :], adjacency_tiles[0, 0], grad_output)
+    )(tile_index[0, 0], tile_count[0], features, weight, bias_vector[None, :], adjacency_tiles[0, 0], grad_output)
     output, grad_features, grad_weight, grad_bias = pl.pallas_call(
         hand_over,
         out_shape=(

time: 105 us -> 103 us (0.981); the launches traced: 104 us -> 103 us
  other arithmetic: 1.26 us -> 0 us
    reduce_min x1 -> x0, other arithmetic: 1.26 us -> none  [on_device(): slots = jnp.min(jnp.where(hit, places, SLOTS), axis=0)]
where the time goes in v3:
time: 103 us
  Pallas kernels  102 us (99%)
  between operations  1.29 us (1%)
    pallas_call x1, Pallas kernels, on_device(): pl.pallas_call(kernel, out_shape=(jax.ShapeDtypeStruct((N, N), BF16), jax...  99.8 us

profile of v3, /device:TPU:8, one launch (start us, length us, event | category | flops | bytes accessed | tf_op | source)
XLA Modules:
  0.0 103.0 jit_solution(713148901809407521)
XLA Ops:
  1.3 99.8 %graph_layer.1 = (bf16[256,256]{1,0:T(8,128)(2,1)}, bf16[256,256]{1,0:T(8,128)(2,1)}, f32[256,256]{1,0:T(8,128)}, f32[1,256]{1,0:T(1,128)}) custom-call(s32[24]{0:T(128)} %bitcast.8, s32[1]{0:T(128)} %bitcast.5.limit, bf16[256,256]{1,0:T(8,128)(2,1)} %features.1, bf16[256,256]{1,0:T(8,128)(2,1)} %weight.1, f32[1,256]{1,0:T(1,128)} %bitcast.7, ...), custom_call_target="tpu_custom_call" | custom-call | tf_op jit(solution)/shard_map/graph_layer/pallas_call | solution.py:720
  101.1 1.9 %hand_over.1 = (bf16[256,256]{1,0:T(8,128)(2,1)}, bf16[256,256]{1,0:T(8,128)(2,1)}, f32[256,256]{1,0:T(8,128)}, f32[1,256]{1,0:T(1,128)}) custom-call(bf16[256,256]{1,0:T(8,128)(2,1)} %get-tuple-element.12.output, bf16[256,256]{1,0:T(8,128)(2,1)} %get-tuple-element.13.grad_features, f32[256,256]{1,0:T(8,128)} %get-tuple-element.14.grad_weight, ...), custom_call_target="tpu_custom_call" | custom-call | tf_op jit(solution)/shard_map/hand_over/pallas_call | solution.py:788

commit v4 on v3

--- a/solution.py
+++ b/solution.py
@@ -353,8 +353,6 @@
         load(part).wait()
     shifted = split_dot(gathered, weight_in[...], (((1,), (0,)), ((), ()))) + bias_in[...]
     sigma = jax.nn.sigmoid(shifted)
-    output_out[...] = (shifted * sigma).astype(BF16)
-    output_store().start()
     signal = (cotangent_in[...].astype(F32) * (sigma * (1.0 + shifted * (1.0 - sigma)))).astype(BF16)
     work[...] = signal
     sig[x * 4 + z, k] = signal.astype(F32).T.astype(BF16)
@@ -394,6 +392,8 @@
         sig_z(1, z).start()
 
     sig_pair(x * 4 + z, k).start()
+    output_out[...] = (shifted * sigma).astype(BF16)
+    output_store().start()
 
     def wa_copy(to, here):
         return remote(wa.at[to], wra.at[here], wa_s.at[to], wa_r.at[here], to * 2 + h, col)
@@ -576,11 +576,10 @@
             shift = pick(s % 4, [0, 2, 3, 1])
             t = ((x + shift) % 4) * 4 + order_near_first(jj, z)
             sig_pair(t, other).wait_recv()
+            both = jnp.concatenate([sig[t, 0], sig[t, 1]], axis=1)
             for c in range(4):
                 slot = slots[t * 4 + c]
-                part = jnp.dot(sig[t, 0], tiles[slot, 0:N, :], preferred_element_type=F32) + jnp.dot(
-                    sig[t, 1], tiles[slot, N:TILE, :], preferred_element_type=F32
-                )
+                part = jnp.dot(both, tiles[slot], preferred_element_type=F32)
                 acc[c, 0] += part[:, 0:N]
                 acc[c, 1] += part[:, N:TILE]
 

time: 103 us -> 103 us (level)
  no operation moved by 1% of the time
where the time goes in v4:
time: 103 us
  Pallas kernels  102 us (99%)
  between operations  1.29 us (1%)
    pallas_call x1, Pallas kernels, on_device(): pl.pallas_call(kernel, out_shape=(jax.ShapeDtypeStruct((N, N), BF16), jax...  99.8 us

profile of v4, /device:TPU:8, one launch (start us, length us, event | category | flops | bytes accessed | tf_op | source)
XLA Modules:
  0.0 103.0 jit_solution(1975206395518014739)
XLA Ops:
  1.3 99.8 %graph_layer.1 = (bf16[256,256]{1,0:T(8,128)(2,1)}, bf16[256,256]{1,0:T(8,128)(2,1)}, f32[256,256]{1,0:T(8,128)}, f32[1,256]{1,0:T(1,128)}) custom-call(s32[24]{0:T(128)} %bitcast.8, s32[1]{0:T(128)} %bitcast.5.limit, bf16[256,256]{1,0:T(8,128)(2,1)} %features.1, bf16[256,256]{1,0:T(8,128)(2,1)} %weight.1, f32[1,256]{1,0:T(1,128)} %bitcast.7, ...), custom_call_target="tpu_custom_call" | custom-call | tf_op jit(solution)/shard_map/graph_layer/pallas_call | solution.py:719
  101.1 1.9 %hand_over.1 = (bf16[256,256]{1,0:T(8,128)(2,1)}, bf16[256,256]{1,0:T(8,128)(2,1)}, f32[256,256]{1,0:T(8,128)}, f32[1,256]{1,0:T(1,128)}) custom-call(bf16[256,256]{1,0:T(8,128)(2,1)} %get-tuple-element.12.output, bf16[256,256]{1,0:T(8,128)(2,1)} %get-tuple-element.13.grad_features, f32[256,256]{1,0:T(8,128)} %get-tuple-element.14.grad_weight, ...), custom_call_target="tpu_custom_call" | custom-call | tf_op jit(solution)/shard_map/hand_over/pallas_call | solution.py:787
